TPU v7x, 128 devices: a whole 4x4x4 slice. The times are simulated.
128 devices in a mesh: ops: 8 (over x, core), sec: 16 (over z, y).
Axes of the slice: x: 4, y: 4, z: 4, core: 2. Of those that a mesh axis runs over, the one named last changes fastest.
Arguments:
- psi: float32 [64, 128, 128], P('sec'), may hold values from -20 to 20
- diag_part: float32 [64, 128, 128], P('sec'), may hold values from 1 to 10
- left_ops: bfloat16 [16384, 128, 128], P(('ops', 'sec')), may hold values from -0.09375 to 0.09375
- right_ops: bfloat16 [16384, 128, 128], P(('ops', 'sec')), may hold values from -0.09375 to 0.09375
- source_sec: int32 [16384], P(('ops', 'sec')), may hold values from 0 to 63
- target_sec: int32 [16384, 1], P(('ops', 'sec')), may hold values from 0 to 63; in each aligned block of 128 rows (0 to 127, 128 to 255, ...) at most 4 rows name the same one
Outputs:
- wave_out: float32 [64, 128, 128], P('sec')
Inputs may be any that keep to these rules, and one draw needn't show every extreme that they name: `target_sec`: among the pairs of one device, no sector is the target of more than 4 pairs, and in every draw some sector is the target of exactly 4.
All inputs are finite; a program needn't handle non-finite values.
Results may differ from a plain program's by a relative error of at most 0.00055.
Values may be sent and summed in bfloat16 or wider, within the bound.
A program may use at most 128 MiB of HBM per device.

v0:
```python
import jax
import jax.numpy as jnp
from jax import lax
from jax.sharding import PartitionSpec as P

ITERS = 3


def shards(psi, diag_part, left_ops, right_ops, source_sec, target_sec):
    owners = lax.axis_size("sec")
    sec_dev, width = (psi.shape[0], psi.shape[1])
    nsec = sec_dev * owners
    pairs_dev = left_ops.shape[0]
    block = min(32, pairs_dev)
    blocks = pairs_dev // block
    targets_all = target_sec[:, 0]
    sector_ids = jnp.arange(nsec, dtype=jnp.int32)
    entries = float(nsec * width * width)
    lefts = left_ops.reshape(blocks, block, width, width)
    rights = right_ops.reshape(blocks, block, width, width)
    sources = source_sec.reshape(blocks, block)
    targets = targets_all.reshape(blocks, block)
    phi = psi
    for step in range(ITERS):
        wave = phi.astype(jnp.bfloat16)
        wave_full = lax.all_gather(wave, "sec", axis=0, tiled=True)

        def step_block(total, items):
            left, right, src, tgt = items
            picked = jnp.take(wave_full, src, axis=0)
            half = jnp.einsum(
                "pij,pjk->pik", left, picked, preferred_element_type=jnp.float32
            ).astype(jnp.bfloat16)
            term = jnp.einsum("pik,plk->pil", half, right, preferred_element_type=jnp.float32)
            onehot = (sector_ids[:, None] == tgt[None, :]).astype(jnp.float32)
            added = jnp.dot(
                onehot,
                term.reshape(block, width * width),
                precision=lax.Precision.HIGHEST,
                preferred_element_type=jnp.float32,
            )
            return (total + added.reshape(nsec, width, width), None)

        start = jnp.zeros((nsec, width, width), jnp.float32)
        partial_sigma, _ = lax.scan(step_block, start, (lefts, rights, sources, targets))
        owned = lax.psum_scatter(partial_sigma, "sec", scatter_dimension=0, tiled=True)
        coupled = lax.psum(owned, "ops")
        sigma = diag_part * phi + coupled
        correlation, weight = lax.psum((jnp.sum(phi * sigma), jnp.sum(phi * phi)), "sec")
        theta = correlation / weight
        fresh = phi - (sigma - theta * phi) / (diag_part + 1.0)
        squares = lax.psum(jnp.sum(fresh * fresh), "sec")
        phi = fresh / jnp.sqrt(squares / entries + 1e-06)
    return phi


def solution(mesh):
    placed = (
        P("sec", None, None),
        P("sec", None, None),
        P(("ops", "sec"), None, None),
        P(("ops", "sec"), None, None),
        P(("ops", "sec")),
        P(("ops", "sec"), None),
    )
    return jax.shard_map(
        shards, mesh=mesh, in_specs=placed, out_specs=P("sec", None, None), check_vma=False
    )
```

profile of v0, /device:TPU:1, one launch (start us, length us, event | category | flops | bytes accessed | tf_op | source)
XLA Modules:
  0.0 961.5 jit_solution(12387730360415734008)
XLA Ops:
  10.9 46.1 %all-gather.4.cloned.1.call-done = bf16[64,128,128]{2,1,0:T(8,128)(2,1)} async-done(((bf16[4,128,128]{2,1,0:T(8,128)(2,1)}), bf16[64,128,128]{2,1,0:T(8,128)(2,1)}) %all-gather.4.cloned.1.call-update) | async-done | bytes 2097168 | tf_op jit(solution)/shard_map/all_gather | solution.py:26
  57.0 48.6 %while.33 = (s32[]{:T(128)}, f32[64,128,128]{2,0,1:T(8,128)}, s32[4,32]{1,0:T(4,128)S(1)}, bf16[4,32,128,128]{3,2,1,0:T(8,128)(2,1)}, s32[4,32]{1,0:T(4,128)S(1)...) while((s32[]{:T(128)}, f32[64,128,128]{2,0,1:T(8,128)}, ...), condition=%wide.region_1.3_spmd.clone, body=%wide.region_0.2_spmd.clone.sunk | while | flops 674237632 | bytes 17831984 | solution.py:45
  72.7 7.5 select_add_fusion.6
  85.4 7.5 select_add_fusion.6
  98.1 7.5 select_add_fusion.6
  105.6 6.6 copy.19
  112.3 76.6 %reduce-scatter.4.cloned.1.call-done = f32[4,128,128]{2,1,0:T(8,128)} async-done(((f32[64,128,128]{2,1,0:T(8,128)}), f32[4,128,128]{2,1,0:T(8,128)}) %reduce-scatter.4.cloned.1.call-update) | async-done | bytes 262160 | tf_op jit(solution)/shard_map/reduce_scatter | solution.py:46
  188.9 60.8 %all-reduce.7.cloned.1.call-done = f32[4,128,128]{2,1,0:T(8,128)} async-done(((f32[4,128,128]{2,1,0:T(8,128)}), f32[4,128,128]{2,1,0:T(8,128)}) %all-reduce.7.cloned.1.call-update) | async-done | bytes 262160 | tf_op jit(solution)/shard_map/psum | solution.py:47
  251.4 34.2 %all-reduce.2 = (f32[]{:T(128)}, f32[]{:T(128)}) all-reduce(f32[]{:T(128)} %get-tuple-element.218, f32[]{:T(128)} %get-tuple-element.217), channel_id=1, replica_groups=mesh['ops'=8,'sec'=16] {'sec'}, use_global_device_ids=true, to_apply=%region_5.7 | all-reduce | flops 2 | bytes 16 | tf_op jit(solution)/shard_map/psum | solution.py:49
  288.6 29.2 %psum.87 = f32[]{:T(128)} all-reduce(f32[]{:T(128)} %get-tuple-element.277), channel_id=1, replica_groups=mesh['ops'=8,'sec'=16] {'sec'}, use_global_device_ids=true, to_apply=%region_9.11 | all-reduce | flops 1 | bytes 8 | tf_op jit(solution)/shard_map/psum | solution.py:52
  319.5 55.4 %all-gather.6.cloned.1.call-done = bf16[64,128,128]{2,1,0:T(8,128)(2,1)} async-done(((bf16[4,128,128]{2,1,0:T(8,128)(2,1)}), bf16[64,128,128]{2,1,0:T(8,128)(2,1)}) %all-gather.6.cloned.1.call-update) | async-done | bytes 2097168 | tf_op jit(solution)/shard_map/all_gather | solution.py:26
  375.0 48.6 %while.34 = (s32[]{:T(128)}, f32[64,128,128]{2,0,1:T(8,128)}, s32[4,32]{1,0:T(4,128)S(1)}, bf16[4,32,128,128]{3,2,1,0:T(8,128)(2,1)}, s32[4,32]{1,0:T(4,128)S(1)...) while((s32[]{:T(128)}, f32[64,128,128]{2,0,1:T(8,128)}, ...), condition=%wide.region_11.13_spmd.clone, body=%wide.region_10.12_spmd.clone.sunk | while | flops 674237632 | bytes 17831984 | solution.py:45
  380.1 5.3 select_add_fusion.7
  390.6 7.5 select_add_fusion.7
  403.3 7.5 select_add_fusion.7
  416.0 7.5 select_add_fusion.7
  423.6 6.6 copy.20
  430.2 76.6 %reduce-scatter.6.cloned.1.call-done = f32[4,128,128]{2,1,0:T(8,128)} async-done(((f32[64,128,128]{2,1,0:T(8,128)}), f32[4,128,128]{2,1,0:T(8,128)}) %reduce-scatter.6.cloned.1.call-update) | async-done | bytes 262160 | tf_op jit(solution)/shard_map/reduce_scatter | solution.py:46
  506.9 60.6 %all-reduce.9.cloned.1.call-done = f32[4,128,128]{2,1,0:T(8,128)} async-done(((f32[4,128,128]{2,1,0:T(8,128)}), f32[4,128,128]{2,1,0:T(8,128)}) %all-reduce.9.cloned.1.call-update) | async-done | bytes 262160 | tf_op jit(solution)/shard_map/psum | solution.py:47
  569.3 34.2 %all-reduce.1 = (f32[]{:T(128)}, f32[]{:T(128)}) all-reduce(f32[]{:T(128)} %get-tuple-element.216, f32[]{:T(128)} %get-tuple-element.215), channel_id=1, replica_groups=mesh['ops'=8,'sec'=16] {'sec'}, use_global_device_ids=true, to_apply=%region_15.17 | all-reduce | flops 2 | bytes 16 | tf_op jit(solution)/shard_map/psum | solution.py:49
  606.5 29.2 %psum.91 = f32[]{:T(128)} all-reduce(f32[]{:T(128)} %get-tuple-element.275), channel_id=1, replica_groups=mesh['ops'=8,'sec'=16] {'sec'}, use_global_device_ids=true, to_apply=%region_19.21 | all-reduce | flops 1 | bytes 8 | tf_op jit(solution)/shard_map/psum | solution.py:52
  637.5 55.4 %all-gather.8.cloned.1.call-done = bf16[64,128,128]{2,1,0:T(8,128)(2,1)} async-done(((bf16[4,128,128]{2,1,0:T(8,128)(2,1)}), bf16[64,128,128]{2,1,0:T(8,128)(2,1)}) %all-gather.8.cloned.1.call-update) | async-done | bytes 2097168 | tf_op jit(solution)/shard_map/all_gather | solution.py:26
  692.9 48.6 %while.35 = (s32[]{:T(128)}, f32[64,128,128]{2,0,1:T(8,128)}, s32[4,32]{1,0:T(4,128)S(1)}, bf16[4,32,128,128]{3,2,1,0:T(8,128)(2,1)}, s32[4,32]{1,0:T(4,128)S(1)...) while((s32[]{:T(128)}, f32[64,128,128]{2,0,1:T(8,128)}, ...), condition=%wide.region_21.23_spmd.clone, body=%wide.region_20.22_spmd.clone.sunk | while | flops 674237632 | bytes 17831984 | solution.py:45
  698.0 5.3 select_add_fusion.8
  708.5 7.5 select_add_fusion.8
  721.2 7.5 select_add_fusion.8
  733.9 7.5 select_add_fusion.8
  741.5 6.6 copy.21
  748.1 76.6 %reduce-scatter.8.cloned.1.call-done = f32[4,128,128]{2,1,0:T(8,128)} async-done(((f32[64,128,128]{2,1,0:T(8,128)}), f32[4,128,128]{2,1,0:T(8,128)}) %reduce-scatter.8.cloned.1.call-update) | async-done | bytes 262160 | tf_op jit(solution)/shard_map/reduce_scatter | solution.py:46
  824.7 60.8 %all-reduce.11.cloned.1.call-done = f32[4,128,128]{2,1,0:T(8,128)} async-done(((f32[4,128,128]{2,1,0:T(8,128)}), f32[4,128,128]{2,1,0:T(8,128)}) %all-reduce.11.cloned.1.call-update) | async-done | bytes 262160 | tf_op jit(solution)/shard_map/psum | solution.py:47
  887.2 34.2 %all-reduce = (f32[]{:T(128)}, f32[]{:T(128)}) all-reduce(f32[]{:T(128)} %get-tuple-element.214, f32[]{:T(128)} %get-tuple-element.213), channel_id=1, replica_groups=mesh['ops'=8,'sec'=16] {'sec'}, use_global_device_ids=true, to_apply=%region_25.27 | all-reduce | flops 2 | bytes 16 | tf_op jit(solution)/shard_map/psum | solution.py:49
  924.4 29.2 %psum.95 = f32[]{:T(128)} all-reduce(f32[]{:T(128)} %get-tuple-element.273), channel_id=1, replica_groups=mesh['ops'=8,'sec'=16] {'sec'}, use_global_device_ids=true, to_apply=%region_29.31 | all-reduce | flops 1 | bytes 8 | tf_op jit(solution)/shard_map/psum | solution.py:52
  (108 shorter events, 84.5 us)
Async XLA Ops:
  6.5 50.5 %all-gather.4.cloned.1.call-start = ((), (), s32[]{:S(2)}) async-start(), calls=%async_computation.3 | async-start | bytes 2228224 | tf_op jit(solution)/shard_map/all_gather | solution.py:26
  8.2 180.6 %reduce-scatter.4.cloned.1.call-start = ((), (), s32[]{:S(2)}) async-start(), calls=%async_computation.4 | async-start | bytes 4456448 | tf_op jit(solution)/shard_map/reduce_scatter | solution.py:46
  112.2 137.5 %copy-start = (f32[4,128,128]{2,1,0:T(8,128)S(1)}, f32[4,128,128]{2,1,0:T(8,128)}, u32[]{:S(2)}) copy-start(f32[4,128,128]{2,1,0:T(8,128)} %param.15) | copy-start | bytes 786436
  112.2 137.5 %copy-start.5 = (f32[4,128,128]{2,1,0:T(8,128)S(1)}, f32[4,128,128]{2,1,0:T(8,128)}, u32[]{:S(2)}) copy-start(f32[4,128,128]{2,1,0:T(8,128)} %param.14) | copy-start | bytes 786436
  112.2 137.5 %all-reduce.7.cloned.1.call-start = ((), (), s32[]{:S(2)}) async-start(), calls=%async_computation.5 | async-start | bytes 524288 | tf_op jit(solution)/shard_map/psum | solution.py:47
  188.8 186.1 %all-gather.6.cloned.1.call-start = ((), (), s32[]{:S(2)}) async-start(), calls=%async_computation.6 | async-start | bytes 2228224 | tf_op jit(solution)/shard_map/all_gather | solution.py:26
  288.6 86.4 %copy-start.3 = (f32[4,128,128]{2,1,0:T(8,128)}, f32[4,128,128]{2,1,0:T(8,128)S(1)}, u32[]{:S(2)}) copy-start(f32[4,128,128]{2,1,0:T(8,128)S(1)} %get-tuple-element.278) | copy-start | bytes 786436
  319.3 187.6 %reduce-scatter.6.cloned.1.call-start = ((), (), s32[]{:S(2)}) async-start(), calls=%async_computation.7 | async-start | bytes 4456448 | tf_op jit(solution)/shard_map/reduce_scatter | solution.py:46
  430.1 137.4 %copy-start.4 = (f32[4,128,128]{2,1,0:T(8,128)S(1)}, f32[4,128,128]{2,1,0:T(8,128)}, u32[]{:S(2)}) copy-start(f32[4,128,128]{2,1,0:T(8,128)} %copy-done.3) | copy-start | bytes 786436
  430.2 137.4 %all-reduce.9.cloned.1.call-start = ((), (), s32[]{:S(2)}) async-start(), calls=%async_computation.8 | async-start | bytes 524288 | tf_op jit(solution)/shard_map/psum | solution.py:47
  506.9 186.0 %all-gather.8.cloned.1.call-start = ((), (), s32[]{:S(2)}) async-start(), calls=%async_computation.9 | async-start | bytes 2228224 | tf_op jit(solution)/shard_map/all_gather | solution.py:26
  606.5 86.4 %copy-start.1 = (f32[4,128,128]{2,1,0:T(8,128)}, f32[4,128,128]{2,1,0:T(8,128)S(1)}, u32[]{:S(2)}) copy-start(f32[4,128,128]{2,1,0:T(8,128)S(1)} %get-tuple-element.276) | copy-start | bytes 786436
  637.2 187.5 %reduce-scatter.8.cloned.1.call-start = ((), (), s32[]{:S(2)}) async-start(), calls=%async_computation.10 | async-start | bytes 4456448 | tf_op jit(solution)/shard_map/reduce_scatter | solution.py:46
  748.0 137.5 %copy-start.2 = (f32[4,128,128]{2,1,0:T(8,128)S(1)}, f32[4,128,128]{2,1,0:T(8,128)}, u32[]{:S(2)}) copy-start(f32[4,128,128]{2,1,0:T(8,128)} %copy-done.1) | copy-start | bytes 786436
  748.1 137.5 %all-reduce.11.cloned.1.call-start = ((), (), s32[]{:S(2)}) async-start(), calls=%async_computation.11 | async-start | bytes 524288 | tf_op jit(solution)/shard_map/psum | solution.py:47
Sparse Core Ops, SparseCore 0:
  9.5 47.4 all-gather.3
  112.3 76.4 reduce-scatter.3
  191.2 58.4 all-reduce.6
  319.4 55.5 all-gather.5
  430.3 76.5 reduce-scatter.5
  509.1 58.3 all-reduce.8
  637.3 55.5 all-gather.7
  748.2 76.4 reduce-scatter.7
  827.1 58.3 all-reduce.10
where the time goes:
time: 979 us; the launch traced here: 962 us
  waiting for transfers between devices  569 us (58%)
  blocking collectives  190 us (19%)
  matrix products  117 us (12%)
  local copies, waits for them, and re-layouts  49.3 us (5%)
  between operations  19.4 us (2%)
  other arithmetic  15.4 us (2%)
    reduce_scatter x3, waiting for transfers between devices, shards(): lax.psum_scatter(partial_sigma, 'sec', scatter_dimension=0, tiled=True)  230 us
    psum x3, waiting for transfers between devices, shards(): coupled = lax.psum(owned, 'ops')  182 us
    all_gather x3, waiting for transfers between devices, shards(): wave_full = lax.all_gather(wave, 'sec', axis=0, tiled=True)  157 us
    psum x3, blocking collectives, shards(): lax.psum((jnp.sum(phi * sigma), jnp.sum(phi * phi)), 'sec')  103 us
    psum x3, blocking collectives, shards(): squares = lax.psum(jnp.sum(fresh * fresh), 'sec')  87.7 us
    dot_general x12, matrix products, step_block(): jnp.dot(onehot, term.reshape(block, width * width), precision=lax.Precisi...  83.7 us
    dot_general x12, matrix products, step_block(): jnp.einsum('pik,plk->pil', half, right, preferred_element_type=jnp.float32)  33.4 us
    gather x12, local copies, waits for them, and re-layouts, step_block(): picked = jnp.take(wave_full, src, axis=0)  28.1 us
  transfers between devices with their start and end apart: 9, of which 9 were waited for; matrix products, arithmetic and copies ran while one was open for 0% of the time, Pallas kernels for 0%

commit v1 on v0

v1 whole, which is shorter than its diff:
```python
import jax
import jax.numpy as jnp
from jax import lax
from jax.experimental import pallas as pl
from jax.experimental.pallas import tpu as pltpu
from jax.sharding import PartitionSpec as P

ITERS = 3
MOST = 4
LAG_SEND = 1
LAG_SUM = 6
B = 128
H = 64
PAIRS = 128
NSEC = 64
MESH = pl.DeviceIdType.MESH


def offset(j):
    return 2 - j + 3 * (j // 2) - 2 * (j // 3)


def inverse(d):
    return jnp.where(d == 0, 3, jnp.where(d == 1, 1, jnp.where(d == 2, 0, 2)))


def position():
    o, i = lax.axis_index("ops"), lax.axis_index("sec")
    return o // 2, lax.rem(o, 2), lax.rem(i, 4), i // 4


def column(row):
    return jnp.broadcast_to(row, (B, B)).T


def pair_tables(source, target, x, y, z):
    ids = lax.broadcasted_iota(jnp.int32, (B, B), 1)
    down = lax.broadcasted_iota(jnp.int32, (B, B), 0)
    part = target // 4
    dx = lax.rem(lax.rem(target, 4) - x + 4, 4)
    dy = lax.rem(lax.rem(part, 4) - y + 4, 4)
    dz = lax.rem(part // 4 - z + 4, 4)
    iy, iz = inverse(dy), inverse(dz)
    odd = lax.rem(dx, 2) == 1
    half = jnp.where(odd, 2 * iy + dx // 2, jnp.where(dx == 2, 0, 4) + iz)
    key = (2 * half + jnp.where(odd, 0, 1)) * 4 + jnp.where(odd, iz, iy)
    other = column(key)
    before = (other == key) & (down < ids)

    def count(mask):
        return jnp.sum(jnp.where(mask, 1, 0), axis=0, keepdims=True)

    rank = count(before)
    place = count((other < key) | before)
    place_col = column(place)
    slot_col = column(key * MOST + rank)
    at = place_col == ids

    def pick(mask, values, empty):
        return empty + jnp.sum(jnp.where(mask, values - empty, 0), axis=0, keepdims=True)

    rows = [pick(at, down, 0), pick(at, column(source), 0)]
    for values in (place_col, down):
        for n in range(2):
            rows.append(pick(slot_col == ids + n * B, values, PAIRS))
    return rows


def kernel(
    source_hbm, target_hbm, psi_hbm, diag_hbm, left_hbm, right_hbm, out_ref,
    left, right, half, wave, pown, psend, precv, rsend, rrecv, mid, msum, acc, phi, diag, weight, csum,
    sc_src, sc_d, sc_own, sc_recv, pairs_in, tab_v, tab,
    lsem, g1s, g1r, g2s, g2r, fws, fwr, pss, psr, rss, rsr, mss, msr, dss, dsr, scs, scr, xs, xr, outs, outr, planes,
):
    x, c, y, z = position()
    me = lax.axis_index("ops")
    sec = z * 4 + y
    mine = sec * 4 + x
    rows = pl.ds(c * H, H)
    sibling = (x * 2 + 1 - c, sec)

    loads = [
        pltpu.make_async_copy(source_hbm, pairs_in.at[pl.ds(0, 1)], lsem.at[0]),
        pltpu.make_async_copy(target_hbm, pairs_in.at[pl.ds(1, 1)], lsem.at[1]),
        pltpu.make_async_copy(psi_hbm.at[:, rows], phi, lsem.at[2]),
        pltpu.make_async_copy(diag_hbm.at[:, rows], diag, lsem.at[3]),
        pltpu.make_async_copy(left_hbm, left, lsem.at[4]),
        pltpu.make_async_copy(right_hbm, right.at[pl.ds(0, PAIRS)], lsem.at[5]),
    ]
    for load in loads:
        load.start()

    def chip(k):
        dx, dy, dz = offset(lax.rem(k, 4)), offset(lax.rem(k // 4, 4)), offset(k // 16)
        return chip_at(dx, dy, dz)

    def chip_at(dx, dy, dz):
        return (lax.rem(x + dx, 4) * 2 + c, lax.rem(z + dz, 4) * 4 + lax.rem(y + dy, 4))

    def owner(h, odd):
        if odd:
            return chip_at(2 - 2 * (h // 4), 0, offset(lax.rem(h, 4)))
        return chip_at(1 + 2 * lax.rem(h, 2), offset(h // 2), 0)

    def place(first, second):
        dy = jnp.where(c == 0, first, second)
        dz = jnp.where(c == 0, second, first)
        return lax.rem(z + dz + 4, 4) * 4 + lax.rem(y + dy + 4, 4)

    barrier = pltpu.get_barrier_semaphore()

    for j in range(1, 4):
        for to in (chip_at(j, 0, 0), chip_at(0, j, 0), chip_at(0, 0, j)):
            pl.semaphore_signal(barrier, inc=1, device_id=to, device_id_type=MESH)
    pl.semaphore_signal(barrier, inc=1, device_id=sibling, device_id_type=MESH)

    right[PAIRS] = jnp.zeros((B, B), jnp.bfloat16)
    half[PAIRS] = jnp.zeros((B, B), jnp.bfloat16)
    loads[0].wait()
    loads[1].wait()
    tab_v[...] = jnp.zeros((8, B), jnp.int32)
    for n, row in enumerate(pair_tables(pairs_in[0:1, :], pairs_in[1:2, :], x, y, z)):
        tab_v[n : n + 1, :] = row
    to_scalar = pltpu.make_async_copy(tab_v, tab, lsem.at[6])
    to_scalar.start()
    loads[2].wait()
    own_sectors = pl.ds(sec * 4, 4)
    wave[own_sectors, rows, :] = phi[...].astype(jnp.bfloat16)
    loads[3].wait()
    weight[...] = 1.0 / (diag[...] + 1.0)
    to_scalar.wait()
    pl.semaphore_wait(barrier, 10)

    def remote(src, dst, s, r, to):
        return pltpu.make_async_remote_copy(
            src_ref=src, dst_ref=dst, send_sem=s, recv_sem=r, device_id=to, device_id_type=MESH
        )

    def sectors(at):
        return wave.at[pl.ds(at * 4, 4), rows]

    def first_copy(j):
        return remote(sectors(sec), sectors(sec), g1s.at[j], g1r.at[j], (me, place(j, 0)))

    def second_copy(j, m):
        block = sectors(place(-j, 0))
        n = j * 4 + m
        return remote(block, block, g2s.at[n], g2r.at[n], (me, place(0, m)))

    def forward_copy(j, m):
        block = sectors(place(-j, -m))
        n = j * 4 + m
        return remote(block, block, fws.at[n], fwr.at[n], sibling)

    def partial_copy(b):
        return remote(psend.at[b], precv.at[b], pss.at[b], psr.at[b], sibling)

    def line_sum_copy(h, odd, kk):
        k = (2 * h + odd) * 4 + kk
        j = offset(kk)
        to = chip_at(0, j, 0) if odd else chip_at(0, 0, j)
        return remote(rsend.at[k], rrecv.at[k], rss.at[k], rsr.at[k], to)

    def owner_copy(h, odd):
        g = 2 * h + odd
        return remote(mid.at[g], msum.at[g], mss.at[g], msr.at[g], owner(h, odd))

    def scalar_copy(k):
        return remote(sc_own, sc_recv.at[k], scs.at[k], scr.at[k], chip(k))

    def line_copy(j):
        to = (lax.rem(x + j, 4) * 2 + c, sec)
        return remote(acc, csum.at[x], xs.at[j], xr.at[j], to)

    def left_products(n):
        picked = wave[tab[1, n]]
        half[n] = jnp.dot(left[tab[0, n]], picked, preferred_element_type=jnp.float32).astype(
            jnp.bfloat16
        )

    def slot(table, k, r):
        return tab[table + k // 32, lax.rem(k, 32) * MOST + r]

    def right_products(b):
        for kk in range(4):
            k = b * 4 + kk
            total = None
            for r in range(0, MOST, 2):
                a = jnp.concatenate([half[slot(2, k, r)], half[slot(2, k, r + 1)]], axis=1)
                w = jnp.concatenate([right[slot(4, k, r)], right[slot(4, k, r + 1)]], axis=1)
                term = lax.dot_general(
                    a, w, (((1,), (1,)), ((), ())), preferred_element_type=jnp.float32
                )
                total = term if total is None else total + term
            low, high = total[:H], total[H:]
            pown[b, kk] = jnp.where(c == 0, low, high)
            psend[b, kk] = jnp.where(c == 0, high, low)
        partial_copy(b).start()

    def send_group(h):
        for odd in range(2):
            g = 2 * h + odd
            partial_copy(g).wait()
            for kk in range(3):
                rsend[g * 4 + kk] = (pown[g, kk] + precv[g, kk]).astype(jnp.bfloat16)
                line_sum_copy(h, odd, kk).start()
            mid[g] = pown[g, 3] + precv[g, 3]

    def sum_group(h):
        for odd in range(2):
            g = 2 * h + odd
            for kk in range(3):
                line_sum_copy(h, odd, kk).wait()
            got = [rrecv[g * 4 + kk].astype(jnp.float32) for kk in range(3)]
            mid[g] = (mid[g] + got[0]) + (got[1] + got[2])
            if not (isinstance(h, int) and g == 15):
                owner_copy(h, odd).start()

    def step(t, theta_before):
        far = (2, 1, 3)
        near = (1, 3, 2)
        for j in far:
            first_copy(j).start()
        for m in far:
            second_copy(0, m).start()
        forward_copy(0, 0).start()
        for j in near:
            first_copy(j).wait_recv()
            for m in far:
                second_copy(j, m).start()
            forward_copy(j, 0).start()
        for j in (0, *near):
            for m in near:
                second_copy(j, m).wait_recv()
                forward_copy(j, m).start()
        for j in near:
            first_copy(j).wait_send()
        for j in range(4):
            for m in near:
                second_copy(j, m).wait_send()
        for j in range(4):
            for m in range(4):
                forward_copy(j, m).wait()

        @pl.when(t == 0)
        def _():
            for j in range(1, 4):
                pl.semaphore_signal(planes, inc=1, device_id=chip_at(j, 0, 0), device_id_type=MESH)
            loads[4].wait()
            loads[5].wait()

        def products(h, with_left):
            for odd in range(2):
                g = 2 * h + odd
                if with_left:
                    for n in range(16):
                        left_products(g * 16 + n)
                right_products(g)

        def early(h, carry):
            products(h, True)

            @pl.when(h >= LAG_SEND)
            def _():
                send_group(h - LAG_SEND)

            return carry

        def late(h, carry):
            products(h, False)
            send_group(h - LAG_SEND)

            @pl.when(h >= LAG_SUM)
            def _():
                sum_group(h - LAG_SUM)

            return carry

        lax.fori_loop(0, 4, early, 0)

        @pl.when(t == 0)
        def _():
            pl.semaphore_wait(planes, 3)

        lax.fori_loop(4, 8, late, 0)
        for h in range(8 - LAG_SEND, 8):
            send_group(h)
        for h in range(8 - LAG_SUM, 8):
            sum_group(h)

        total = mid[15]
        for h in range(8):
            for odd in range(2):
                if 2 * h + odd < 15:
                    owner_copy(h, odd).wait()
                    total += msum[2 * h + odd]
        acc[...] = total
        for j in range(1, 4):
            line_copy(j).start()

        now = phi[x]
        csum[x] = total
        sigma = diag[x] * now + total
        ua = now * weight[x]
        fa = now - (sigma - theta_before * now) * weight[x]
        lane = lax.broadcasted_iota(jnp.int32, (1, B), 1)
        row = jnp.zeros((1, B), jnp.float32)
        for j, terms in enumerate((now * sigma, now * now, fa * fa, fa * ua, ua * ua)):
            value = jnp.sum(jnp.sum(terms, axis=0, keepdims=True), axis=1, keepdims=True)
            row = jnp.where(lane == j, value, row)
        sc_src[...] = row
        swap = remote(sc_src, sc_d, dss.at[0], dsr.at[0], sibling)
        swap.start()
        swap.wait()
        sc_own[...] = row + sc_d[...]

        def send_scalars(k, carry):
            scalar_copy(k).start()
            return carry

        def wait_scalars(k, carry):
            scalar_copy(k).wait()
            return carry

        lax.fori_loop(0, NSEC - 1, send_scalars, 0)
        sc_recv[NSEC - 1] = sc_own[...]
        lax.fori_loop(0, NSEC - 1, wait_scalars, 0)
        sums = jnp.sum(sc_recv[...], axis=0)
        theta = sums[:, 0:1] / sums[:, 1:2]
        delta = theta - theta_before
        squares = sums[:, 2:3] + delta * (2.0 * sums[:, 3:4] + delta * sums[:, 4:5])
        scale = 1.0 / jnp.sqrt(squares / float(NSEC * B * B) + 1e-06)
        for j in range(1, 4):
            line_copy(j).wait()
        for j in range(4):
            now = phi[j]
            fresh = now - (diag[j] * now + csum[j] - theta * now) * weight[j]
            new = fresh * scale
            phi[j] = new
            wave[sec * 4 + j, rows, :] = new.astype(jnp.bfloat16)
        return theta

    lax.fori_loop(0, ITERS, step, jnp.zeros((1, 1), jnp.float32))

    out_ref[:, rows, :] = phi[...]
    last = remote(phi, out_ref.at[:, rows], outs.at[0], outr.at[0], sibling)
    last.start()
    last.wait()


def shards(psi, diag_part, left_ops, right_ops, source_sec, target_sec):
    vmem = pl.BlockSpec(memory_space=pltpu.VMEM)
    hbm = pl.BlockSpec(memory_space=pl.ANY)
    f32, bf16 = jnp.float32, jnp.bfloat16
    dma = pltpu.SemaphoreType.DMA
    quarter = pltpu.VMEM((4, H, B), f32)
    line = pltpu.VMEM((1, B), f32)
    partial = pltpu.VMEM((16, 4, H, B), f32)
    packed = pltpu.VMEM((NSEC, H, B), bf16)
    return pl.pallas_call(
        kernel,
        out_shape=jax.ShapeDtypeStruct((4, B, B), f32),
        in_specs=[hbm] * 6,
        out_specs=vmem,
        scratch_shapes=[
            pltpu.VMEM((PAIRS, B, B), bf16),
            pltpu.VMEM((PAIRS + 1, B, B), bf16),
            pltpu.VMEM((PAIRS + 1, B, B), bf16),
            pltpu.VMEM((NSEC, B, B), bf16),
            partial,
            partial,
            partial,
            packed,
            packed,
            pltpu.VMEM((16, H, B), f32),
            pltpu.VMEM((16, H, B), f32),
            pltpu.VMEM((H, B), f32),
            quarter,
            quarter,
            quarter,
            quarter,
            line,
            line,
            line,
            pltpu.VMEM((NSEC, 1, B), f32),
            pltpu.VMEM((8, B), jnp.int32),
            pltpu.VMEM((8, B), jnp.int32),
            pltpu.SMEM((8, B), jnp.int32),
            dma((7,)),
            dma((4,)),
            dma((4,)),
            dma((16,)),
            dma((16,)),
            dma((16,)),
            dma((16,)),
            dma((16,)),
            dma((16,)),
            dma((NSEC,)),
            dma((NSEC,)),
            dma((16,)),
            dma((16,)),
            dma((1,)),
            dma((1,)),
            dma((NSEC,)),
            dma((NSEC,)),
            dma((4,)),
            dma((4,)),
            dma((1,)),
            dma((1,)),
            pltpu.SemaphoreType.REGULAR,
        ],
        compiler_params=pltpu.CompilerParams(
            collective_id=0, has_side_effects=True, vmem_limit_bytes=62 << 20
        ),
        cost_estimate=pl.CostEstimate(
            flops=ITERS * PAIRS * 4 * B * B * B, bytes_accessed=9 << 20, transcendentals=0
        ),
        name="davidson",
    )(
        source_sec.reshape(1, PAIRS), target_sec.reshape(1, PAIRS), psi, diag_part, left_ops,
        right_ops,
    )


def solution(mesh):
    placed = (
        P("sec", None, None),
        P("sec", None, None),
        P(("ops", "sec"), None, None),
        P(("ops", "sec"), None, None),
        P(("ops", "sec")),
        P(("ops", "sec"), None),
    )
    return jax.shard_map(
        shards, mesh=mesh, in_specs=placed, out_specs=P("sec", None, None), check_vma=False
    )
```

time: 979 us -> 133 us (0.14); the launches traced: 962 us -> 133 us
  waiting for transfers between devices: 569 us -> 0 us
  blocking collectives: 190 us -> 0 us
  Pallas kernels: 0 us -> 131 us
  matrix products: 117 us -> 0 us
  local copies, waits for them, and re-layouts: 49.3 us -> 1.67 us
  between operations: 19.4 us -> 0.01 us
  other arithmetic: 15.4 us -> 0 us
    reduce_scatter x3 -> x0, waiting for transfers between devices: 230 us -> none  [shards(): lax.psum_scatter(partial_sigma, 'sec', scatter_dimension=0, tiled=True)]
    psum x6 -> x0, blocking collectives: 190 us -> none  [the longest x3 103 us: shards(): lax.psum((jnp.sum(phi * sigma), jnp.sum(phi * phi)), 'sec')]
    psum x3 -> x0, waiting for transfers between devices: 182 us -> none  [shards(): coupled = lax.psum(owned, 'ops')]
    all_gather x3 -> x0, waiting for transfers between devices: 157 us -> none  [shards(): wave_full = lax.all_gather(wave, 'sec', axis=0, tiled=True)]
    pallas_call x0 -> x1, Pallas kernels: none -> 131 us  [shards(): pl.pallas_call(kernel, out_shape=jax.ShapeDtypeStruct((4, B, B), f32), in...]
    dot_general x24 -> x0, matrix products: 117 us -> none  [the longest x12 83.7 us: step_block(): jnp.dot(onehot, term.reshape(block, width * width), precision=lax.Precisi...]
    gather x12 -> x0, local copies, waits for them, and re-layouts: 28.1 us -> none  [step_block(): picked = jnp.take(wave_full, src, axis=0)]
    while x3 -> x0, local copies, waits for them, and re-layouts: 19.8 us -> none  [shards(): lax.scan(step_block, start, (lefts, rights, sources, targets))]
  transfers between devices with their start and end apart: 9 -> 0, of which waited for: 9 -> 0; matrix products, arithmetic and copies ran while one was open for 0% -> 0% of each run, Pallas kernels for 0% -> 0%
where the time goes in v1:
time: 133 us
  Pallas kernels  131 us (98%)
  local copies, waits for them, and re-layouts  1.67 us (1%)
    pallas_call x1, Pallas kernels, shards(): pl.pallas_call(kernel, out_shape=jax.ShapeDtypeStruct((4, B, B), f32), in...  131 us

profile of v1, /device:TPU:1, one launch (start us, length us, event | category | flops | bytes accessed | tf_op | source)
XLA Modules:
  0.0 132.9 jit_solution(1401865774496665475)
XLA Ops:
  0.0 131.2 %davidson.1 = f32[4,128,128]{2,1,0:T(8,128)} custom-call(s32[1,128]{1,0:T(1,128)} %bitcast.2, s32[1,128]{1,0:T(1,128)} %bitcast.3, f32[4,128,128]{2,1,0:T(8,128)} %psi_hbm.1, f32[4,128,128]{2,1,0:T(8,128)} %diag_hbm.1, bf16[128,128,128]{2,1,0:T(8,128)(2,1)} %left_hbm.1, bf16[128,128,128]{2,1,0:T(8,128)(2,1)} %right_hbm.1), custom_call_target="tpu_custom_call" | custom-call | flops 3221225472 | bytes 9437184 | tf_op jit(solution)/shard_map/davidson/pallas_call | solution.py:360
  131.2 1.7 %copy.8 = f32[4,128,128]{2,1,0:T(8,128)} copy(f32[4,128,128]{2,1,0:T(8,128)} %davidson.1) | data formatting | bytes 524288

commit v2 on v1

--- a/solution.py
+++ b/solution.py
@@ -7,8 +7,8 @@
 
 ITERS = 3
 MOST = 4
-LAG_SEND = 1
-LAG_SUM = 6
+TURNS, EACH = 8, 8
+GROUPS = 8
 B = 128
 H = 64
 PAIRS = 128
@@ -16,12 +16,25 @@
 MESH = pl.DeviceIdType.MESH
 
 
-def offset(j):
-    return 2 - j + 3 * (j // 2) - 2 * (j // 3)
-
-
-def inverse(d):
-    return jnp.where(d == 0, 3, jnp.where(d == 1, 1, jnp.where(d == 2, 0, 2)))
+ORDER = [
+    42, 38, 46, 34, 41, 25, 57, 9, 26, 22, 30, 18, 43, 27, 59, 11,
+    58, 54, 62, 50, 37, 21, 53, 5, 10, 6, 14, 2, 40, 24, 56, 8,
+    39, 45, 47, 23, 61, 29, 55, 31, 63, 33, 36, 35, 44, 7, 13, 15,
+    17, 52, 20, 49, 19, 60, 28, 51, 32, 1, 4, 3, 12, 16, 48, 0,
+]
+WORDS = [
+    sum(place * NSEC**n for n, place in enumerate(ORDER[at : at + 5])) for at in range(0, NSEC, 5)
+]
+
+
+def place_of(k):
+    word = jnp.int32(WORDS[0])
+    for n in range(1, len(WORDS)):
+        word = jnp.where(k // 5 == n, jnp.int32(WORDS[n]), word)
+    scale = jnp.int32(1)
+    for n in range(1, 5):
+        scale = jnp.where(lax.rem(k, 5) == n, jnp.int32(NSEC**n), scale)
+    return lax.rem(word // scale, NSEC)
 
 
 def position():
@@ -40,10 +53,10 @@
     dx = lax.rem(lax.rem(target, 4) - x + 4, 4)
     dy = lax.rem(lax.rem(part, 4) - y + 4, 4)
     dz = lax.rem(part // 4 - z + 4, 4)
-    iy, iz = inverse(dy), inverse(dz)
-    odd = lax.rem(dx, 2) == 1
-    half = jnp.where(odd, 2 * iy + dx // 2, jnp.where(dx == 2, 0, 4) + iz)
-    key = (2 * half + jnp.where(odd, 0, 1)) * 4 + jnp.where(odd, iz, iy)
+    seen = dx + 4 * dy + 16 * dz
+    key = jnp.zeros_like(seen)
+    for n, at in enumerate(ORDER):
+        key = jnp.where(seen == at, n, key)
     other = column(key)
     before = (other == key) & (down < ids)
 
@@ -91,16 +104,11 @@
         load.start()
 
     def chip(k):
-        dx, dy, dz = offset(lax.rem(k, 4)), offset(lax.rem(k // 4, 4)), offset(k // 16)
-        return chip_at(dx, dy, dz)
+        q = place_of(k)
+        return chip_at(lax.rem(q, 4), lax.rem(q // 4, 4), q // 16)
 
     def chip_at(dx, dy, dz):
         return (lax.rem(x + dx, 4) * 2 + c, lax.rem(z + dz, 4) * 4 + lax.rem(y + dy, 4))
-
-    def owner(h, odd):
-        if odd:
-            return chip_at(2 - 2 * (h // 4), 0, offset(lax.rem(h, 4)))
-        return chip_at(1 + 2 * lax.rem(h, 2), offset(h // 2), 0)
 
     def place(first, second):
         dy = jnp.where(c == 0, first, second)
@@ -114,21 +122,8 @@
             pl.semaphore_signal(barrier, inc=1, device_id=to, device_id_type=MESH)
     pl.semaphore_signal(barrier, inc=1, device_id=sibling, device_id_type=MESH)
 
-    right[PAIRS] = jnp.zeros((B, B), jnp.bfloat16)
-    half[PAIRS] = jnp.zeros((B, B), jnp.bfloat16)
-    loads[0].wait()
-    loads[1].wait()
-    tab_v[...] = jnp.zeros((8, B), jnp.int32)
-    for n, row in enumerate(pair_tables(pairs_in[0:1, :], pairs_in[1:2, :], x, y, z)):
-        tab_v[n : n + 1, :] = row
-    to_scalar = pltpu.make_async_copy(tab_v, tab, lsem.at[6])
-    to_scalar.start()
     loads[2].wait()
-    own_sectors = pl.ds(sec * 4, 4)
-    wave[own_sectors, rows, :] = phi[...].astype(jnp.bfloat16)
-    loads[3].wait()
-    weight[...] = 1.0 / (diag[...] + 1.0)
-    to_scalar.wait()
+    wave[pl.ds(sec * 4, 4), rows, :] = phi[...].astype(jnp.bfloat16)
     pl.semaphore_wait(barrier, 10)
 
     def remote(src, dst, s, r, to):
@@ -155,18 +150,21 @@
     def partial_copy(b):
         return remote(psend.at[b], precv.at[b], pss.at[b], psr.at[b], sibling)
 
-    def line_sum_copy(h, odd, kk):
-        k = (2 * h + odd) * 4 + kk
-        j = offset(kk)
-        to = chip_at(0, j, 0) if odd else chip_at(0, 0, j)
+    def line_sum_copy(g, kk):
+        k = g * 4 + kk
+        q = place_of(k)
+        across = jnp.where(lax.rem(q, 4) == 2, 1, 0)
+        to = chip_at(0, across * lax.rem(q // 4, 4), (1 - across) * (q // 16))
         return remote(rsend.at[k], rrecv.at[k], rss.at[k], rsr.at[k], to)
 
-    def owner_copy(h, odd):
-        g = 2 * h + odd
-        return remote(mid.at[g], msum.at[g], mss.at[g], msr.at[g], owner(h, odd))
+    def plane_sum_copy(g):
+        return remote(mid.at[g], msum.at[g], mss.at[g], msr.at[g], chip(g * 4 + 3))
+
+    def sum_copy(k):
+        return remote(rsend.at[k], rrecv.at[k], rss.at[k], rsr.at[k], chip(k))
 
     def scalar_copy(k):
-        return remote(sc_own, sc_recv.at[k], scs.at[k], scr.at[k], chip(k))
+        return remote(sc_own, sc_recv.at[mine], scs.at[k], scr.at[k], chip(k))
 
     def line_copy(j):
         to = (lax.rem(x + j, 4) * 2 + c, sec)
@@ -181,9 +179,9 @@
     def slot(table, k, r):
         return tab[table + k // 32, lax.rem(k, 32) * MOST + r]
 
-    def right_products(b):
-        for kk in range(4):
-            k = b * 4 + kk
+    def right_products(h):
+        for i in range(EACH):
+            k = h * EACH + i
             total = None
             for r in range(0, MOST, 2):
                 a = jnp.concatenate([half[slot(2, k, r)], half[slot(2, k, r + 1)]], axis=1)
@@ -193,28 +191,58 @@
                 )
                 total = term if total is None else total + term
             low, high = total[:H], total[H:]
-            pown[b, kk] = jnp.where(c == 0, low, high)
-            psend[b, kk] = jnp.where(c == 0, high, low)
-        partial_copy(b).start()
-
-    def send_group(h):
-        for odd in range(2):
-            g = 2 * h + odd
-            partial_copy(g).wait()
+            pown[h, i] = jnp.where(c == 0, low, high)
+            psend[h, i] = jnp.where(c == 0, high, low)
+        partial_copy(h).start()
+
+    def send_lines(h):
+        partial_copy(h).wait()
+        for i in range(EACH):
+            both = pown[h, i] + precv[h, i]
+            g, kk = 2 * h + i // 4, i % 4
+            if kk == 3:
+                mid[g] = both
+            else:
+                rsend[g * 4 + kk] = both.astype(jnp.bfloat16)
+                line_sum_copy(g, kk).start()
+
+    def sum_lines(h):
+        for n in range(2):
+            g = 2 * h + n
             for kk in range(3):
-                rsend[g * 4 + kk] = (pown[g, kk] + precv[g, kk]).astype(jnp.bfloat16)
-                line_sum_copy(h, odd, kk).start()
-            mid[g] = pown[g, 3] + precv[g, 3]
-
-    def sum_group(h):
-        for odd in range(2):
-            g = 2 * h + odd
-            for kk in range(3):
-                line_sum_copy(h, odd, kk).wait()
+                line_sum_copy(g, kk).wait_recv()
             got = [rrecv[g * 4 + kk].astype(jnp.float32) for kk in range(3)]
             mid[g] = (mid[g] + got[0]) + (got[1] + got[2])
-            if not (isinstance(h, int) and g == 15):
-                owner_copy(h, odd).start()
+            plane_sum_copy(g).start()
+
+    def send_straight(h):
+        partial_copy(h).wait()
+        for i in range(EACH):
+            both = pown[h, i] + precv[h, i]
+            if isinstance(h, int) and h == TURNS - 1 and i == EACH - 1:
+                acc[...] = both
+            else:
+                rsend[h * EACH + i] = both.astype(jnp.bfloat16)
+                sum_copy(h * EACH + i).start()
+
+    def prepare():
+        right[PAIRS] = jnp.zeros((B, B), jnp.bfloat16)
+        half[PAIRS] = jnp.zeros((B, B), jnp.bfloat16)
+        loads[0].wait()
+        loads[1].wait()
+        tab_v[...] = jnp.zeros((8, B), jnp.int32)
+        for n, row in enumerate(pair_tables(pairs_in[0:1, :], pairs_in[1:2, :], x, y, z)):
+            tab_v[n : n + 1, :] = row
+        to_scalar = pltpu.make_async_copy(tab_v, tab, lsem.at[6])
+        to_scalar.start()
+        loads[3].wait()
+        weight[...] = 1.0 / (diag[...] + 1.0)
+        to_scalar.wait()
+
+    def scalars_sent(n, carry):
+        for m in range(9):
+            scalar_copy(n * 9 + m).wait_send()
+        return carry
 
     def step(t, theta_before):
         far = (2, 1, 3)
@@ -224,6 +252,15 @@
         for m in far:
             second_copy(0, m).start()
         forward_copy(0, 0).start()
+
+        @pl.when(t == 0)
+        def _():
+            prepare()
+
+        @pl.when(t > 0)
+        def _():
+            lax.fori_loop(0, 7, scalars_sent, 0)
+
         for j in near:
             first_copy(j).wait_recv()
             for m in far:
@@ -233,14 +270,9 @@
             for m in near:
                 second_copy(j, m).wait_recv()
                 forward_copy(j, m).start()
-        for j in near:
-            first_copy(j).wait_send()
-        for j in range(4):
-            for m in near:
-                second_copy(j, m).wait_send()
-        for j in range(4):
-            for m in range(4):
-                forward_copy(j, m).wait()
+        for j in (0, *near):
+            for m in (0, *near):
+                forward_copy(j, m).wait_recv()
 
         @pl.when(t == 0)
         def _():
@@ -249,51 +281,66 @@
             loads[4].wait()
             loads[5].wait()
 
-        def products(h, with_left):
-            for odd in range(2):
-                g = 2 * h + odd
-                if with_left:
-                    for n in range(16):
-                        left_products(g * 16 + n)
-                right_products(g)
-
         def early(h, carry):
-            products(h, True)
-
-            @pl.when(h >= LAG_SEND)
-            def _():
-                send_group(h - LAG_SEND)
-
+            right_products(h)
+            for n in range(32):
+                left_products((h + 1) * 32 + n)
+            return carry
+
+        def middle(h, carry):
+            right_products(h)
+            send_lines(h - 2)
             return carry
 
         def late(h, carry):
-            products(h, False)
-            send_group(h - LAG_SEND)
-
-            @pl.when(h >= LAG_SUM)
-            def _():
-                sum_group(h - LAG_SUM)
-
-            return carry
-
-        lax.fori_loop(0, 4, early, 0)
+            right_products(h)
+            send_straight(h - 2)
+            return carry
+
+        for n in range(32):
+            left_products(n)
+        lax.fori_loop(0, 3, early, 0)
+        send_lines(0)
+        lax.fori_loop(3, 6, middle, 0)
 
         @pl.when(t == 0)
         def _():
             pl.semaphore_wait(planes, 3)
 
-        lax.fori_loop(4, 8, late, 0)
-        for h in range(8 - LAG_SEND, 8):
-            send_group(h)
-        for h in range(8 - LAG_SUM, 8):
-            sum_group(h)
-
-        total = mid[15]
-        for h in range(8):
-            for odd in range(2):
-                if 2 * h + odd < 15:
-                    owner_copy(h, odd).wait()
-                    total += msum[2 * h + odd]
+        lax.fori_loop(6, TURNS, late, 0)
+        sum_lines(0)
+        send_straight(TURNS - 2)
+        sum_lines(1)
+        send_straight(TURNS - 1)
+        sum_lines(2)
+        sum_lines(3)
+
+        for j in (0, *near):
+            if j:
+                first_copy(j).wait_send()
+            for m in (0, *near):
+                if m:
+                    second_copy(j, m).wait_send()
+                forward_copy(j, m).wait_send()
+
+        def collect(n, carry):
+            got = []
+            for m in range(8):
+                k = GROUPS * 4 + n * 8 + m
+                sum_copy(k).wait_recv()
+                got.append(rrecv[k].astype(jnp.float32))
+            pairs = [got[m] + got[m + 1] for m in range(0, 8, 2)]
+            acc[...] += (pairs[0] + pairs[1]) + (pairs[2] + pairs[3])
+            return carry
+
+        lax.fori_loop(0, 3, collect, 0)
+        total = acc[...]
+        for k in range(NSEC - 8, NSEC - 1):
+            sum_copy(k).wait_recv()
+            total += rrecv[k].astype(jnp.float32)
+        for g in range(GROUPS):
+            plane_sum_copy(g).wait_recv()
+            total += msum[g]
         acc[...] = total
         for j in range(1, 4):
             line_copy(j).start()
@@ -314,17 +361,25 @@
         swap.wait()
         sc_own[...] = row + sc_d[...]
 
-        def send_scalars(k, carry):
-            scalar_copy(k).start()
-            return carry
-
-        def wait_scalars(k, carry):
-            scalar_copy(k).wait()
-            return carry
-
-        lax.fori_loop(0, NSEC - 1, send_scalars, 0)
-        sc_recv[NSEC - 1] = sc_own[...]
-        lax.fori_loop(0, NSEC - 1, wait_scalars, 0)
+        def send_scalars(n, carry):
+            for m in range(9):
+                scalar_copy(n * 9 + m).start()
+            return carry
+
+        def wait_scalars(n, carry):
+            for m in range(9):
+                scalar_copy(n * 9 + m).wait_recv()
+            return carry
+
+        lax.fori_loop(0, 7, send_scalars, 0)
+        sc_recv[mine] = sc_own[...]
+        for g in range(GROUPS):
+            for kk in range(3):
+                line_sum_copy(g, kk).wait_send()
+            plane_sum_copy(g).wait_send()
+        for k in range(GROUPS * 4, NSEC - 1):
+            sum_copy(k).wait_send()
+        lax.fori_loop(0, 7, wait_scalars, 0)
         sums = jnp.sum(sc_recv[...], axis=0)
         theta = sums[:, 0:1] / sums[:, 1:2]
         delta = theta - theta_before
@@ -341,6 +396,7 @@
         return theta
 
     lax.fori_loop(0, ITERS, step, jnp.zeros((1, 1), jnp.float32))
+    lax.fori_loop(0, 7, scalars_sent, 0)
 
     out_ref[:, rows, :] = phi[...]
     last = remote(phi, out_ref.at[:, rows], outs.at[0], outr.at[0], sibling)
@@ -355,7 +411,7 @@
     dma = pltpu.SemaphoreType.DMA
     quarter = pltpu.VMEM((4, H, B), f32)
     line = pltpu.VMEM((1, B), f32)
-    partial = pltpu.VMEM((16, 4, H, B), f32)
+    partial = pltpu.VMEM((TURNS, EACH, H, B), f32)
     packed = pltpu.VMEM((NSEC, H, B), bf16)
     return pl.pallas_call(
         kernel,
@@ -372,8 +428,8 @@
             partial,
             packed,
             packed,
-            pltpu.VMEM((16, H, B), f32),
-            pltpu.VMEM((16, H, B), f32),
+            pltpu.VMEM((GROUPS, H, B), f32),
+            pltpu.VMEM((GROUPS, H, B), f32),
             pltpu.VMEM((H, B), f32),
             quarter,
             quarter,
@@ -397,8 +453,8 @@
             dma((16,)),
             dma((NSEC,)),
             dma((NSEC,)),
-            dma((16,)),
-            dma((16,)),
+            dma((GROUPS,)),
+            dma((GROUPS,)),
             dma((1,)),
             dma((1,)),
             dma((NSEC,)),

time: 133 us -> 131 us (0.985)
    pallas_call x1, Pallas kernels: 131 us -> 130 us  [shards(): pl.pallas_call(kernel, out_shape=jax.ShapeDtypeStruct((4, B, B), f32), in...]
where the time goes in v2:
time: 131 us
  Pallas kernels  130 us (99%)
  local copies, waits for them, and re-layouts  1.67 us (1%)
    pallas_call x1, Pallas kernels, shards(): pl.pallas_call(kernel, out_shape=jax.ShapeDtypeStruct((4, B, B), f32), in...  130 us

profile of v2, /device:TPU:1, one launch (start us, length us, event | category | flops | bytes accessed | tf_op | source)
XLA Modules:
  0.0 131.3 jit_solution(606592908572027506)
XLA Ops:
  0.0 129.6 %davidson.1 = f32[4,128,128]{2,1,0:T(8,128)} custom-call(s32[1,128]{1,0:T(1,128)} %bitcast.2, s32[1,128]{1,0:T(1,128)} %bitcast.3, f32[4,128,128]{2,1,0:T(8,128)} %psi_hbm.1, f32[4,128,128]{2,1,0:T(8,128)} %diag_hbm.1, bf16[128,128,128]{2,1,0:T(8,128)(2,1)} %left_hbm.1, bf16[128,128,128]{2,1,0:T(8,128)(2,1)} %right_hbm.1), custom_call_target="tpu_custom_call" | custom-call | flops 3221225472 | bytes 9437184 | tf_op jit(solution)/shard_map/davidson/pallas_call | solution.py:416
  129.6 1.7 %copy.8 = f32[4,128,128]{2,1,0:T(8,128)} copy(f32[4,128,128]{2,1,0:T(8,128)} %davidson.1) | data formatting | bytes 524288

commit v3 on v2

--- a/solution.py
+++ b/solution.py
@@ -17,14 +17,18 @@
 
 
 ORDER = [
-    42, 38, 46, 34, 41, 25, 57, 9, 26, 22, 30, 18, 43, 27, 59, 11,
-    58, 54, 62, 50, 37, 21, 53, 5, 10, 6, 14, 2, 40, 24, 56, 8,
-    39, 45, 47, 23, 61, 29, 55, 31, 63, 33, 36, 35, 44, 7, 13, 15,
-    17, 52, 20, 49, 19, 60, 28, 51, 32, 1, 4, 3, 12, 16, 48, 0,
+    38, 37, 39, 36, 26, 22, 30, 18, 41, 25, 57, 9, 46, 45, 47, 44,
+    58, 54, 62, 50, 43, 27, 59, 11, 34, 33, 35, 32, 10, 6, 14, 2,
+    42, 40, 21, 63, 23, 61, 29, 55, 31, 53, 24, 56, 17, 51, 5, 15,
+    19, 49, 7, 13, 20, 60, 28, 52, 8, 1, 3, 16, 48, 4, 12, 0,
 ]
 WORDS = [
     sum(place * NSEC**n for n, place in enumerate(ORDER[at : at + 5])) for at in range(0, NSEC, 5)
 ]
+
+
+def offset(kk):
+    return (2, 1, 3, 0)[kk]
 
 
 def place_of(k):
@@ -152,9 +156,8 @@
 
     def line_sum_copy(g, kk):
         k = g * 4 + kk
-        q = place_of(k)
-        across = jnp.where(lax.rem(q, 4) == 2, 1, 0)
-        to = chip_at(0, across * lax.rem(q // 4, 4), (1 - across) * (q // 16))
+        axis = lax.rem(g, 3)
+        to = chip_at(*(jnp.where(axis == n, offset(kk), 0) for n in range(3)))
         return remote(rsend.at[k], rrecv.at[k], rss.at[k], rsr.at[k], to)
 
     def plane_sum_copy(g):

time: 131 us -> 127 us (0.969)
  Pallas kernels: 130 us -> 125 us
    pallas_call x1, Pallas kernels: 130 us -> 125 us  [shards(): pl.pallas_call(kernel, out_shape=jax.ShapeDtypeStruct((4, B, B), f32), in...]
where the time goes in v3:
time: 127 us
  Pallas kernels  125 us (98%)
  local copies, waits for them, and re-layouts  1.67 us (1%)
    pallas_call x1, Pallas kernels, shards(): pl.pallas_call(kernel, out_shape=jax.ShapeDtypeStruct((4, B, B), f32), in...  125 us

profile of v3, /device:TPU:1, one launch (start us, length us, event | category | flops | bytes accessed | tf_op | source)
XLA Modules:
  0.0 126.9 jit_solution(1849953662950314299)
XLA Ops:
  0.0 125.2 %davidson.1 = f32[4,128,128]{2,1,0:T(8,128)} custom-call(s32[1,128]{1,0:T(1,128)} %bitcast.2, s32[1,128]{1,0:T(1,128)} %bitcast.3, f32[4,128,128]{2,1,0:T(8,128)} %psi_hbm.1, f32[4,128,128]{2,1,0:T(8,128)} %diag_hbm.1, bf16[128,128,128]{2,1,0:T(8,128)(2,1)} %left_hbm.1, bf16[128,128,128]{2,1,0:T(8,128)(2,1)} %right_hbm.1), custom_call_target="tpu_custom_call" | custom-call | flops 3221225472 | bytes 9437184 | tf_op jit(solution)/shard_map/davidson/pallas_call | solution.py:419
  125.2 1.7 %copy.8 = f32[4,128,128]{2,1,0:T(8,128)} copy(f32[4,128,128]{2,1,0:T(8,128)} %davidson.1) | data formatting | bytes 524288

commit v4 on v3

--- a/solution.py
+++ b/solution.py
@@ -9,6 +9,8 @@
 MOST = 4
 TURNS, EACH = 8, 8
 GROUPS = 8
+SHARED = (0, 1)
+WHOLE = tuple(j for j in (0, 1, 3, 2) if j not in SHARED)
 B = 128
 H = 64
 PAIRS = 128
@@ -87,7 +89,7 @@
     source_hbm, target_hbm, psi_hbm, diag_hbm, left_hbm, right_hbm, out_ref,
     left, right, half, wave, pown, psend, precv, rsend, rrecv, mid, msum, acc, phi, diag, weight, csum,
     sc_src, sc_d, sc_own, sc_recv, pairs_in, tab_v, tab,
-    lsem, g1s, g1r, g2s, g2r, fws, fwr, pss, psr, rss, rsr, mss, msr, dss, dsr, scs, scr, xs, xr, outs, outr, planes,
+    lsem, g1s, g1r, g2s, g2r, g3s, g3r, fws, fwr, pss, psr, rss, rsr, mss, msr, dss, dsr, scs, scr, xs, xr, outs, outr, planes,
 ):
     x, c, y, z = position()
     me = lax.axis_index("ops")
@@ -138,13 +140,22 @@
     def sectors(at):
         return wave.at[pl.ds(at * 4, 4), rows]
 
+    def two_sectors(at):
+        return wave.at[pl.ds(at * 4 + 2 * lax.rem(x, 2), 2), rows]
+
     def first_copy(j):
         return remote(sectors(sec), sectors(sec), g1s.at[j], g1r.at[j], (me, place(j, 0)))
 
     def second_copy(j, m):
-        block = sectors(place(-j, 0))
+        block = two_sectors(place(-j, 0)) if j in SHARED else sectors(place(-j, 0))
         n = j * 4 + m
         return remote(block, block, g2s.at[n], g2r.at[n], (me, place(0, m)))
+
+    def share_copy(j, m):
+        block = two_sectors(place(-j, -m))
+        n = j * 4 + m
+        to = lax.rem(x + 3 + 2 * lax.rem(x + j + m + 1, 2), 4) * 2 + c
+        return remote(block, block, g3s.at[n], g3r.at[n], (to, sec))
 
     def forward_copy(j, m):
         block = sectors(place(-j, -m))
@@ -228,6 +239,8 @@
                 rsend[h * EACH + i] = both.astype(jnp.bfloat16)
                 sum_copy(h * EACH + i).start()
 
+    to_scalar = pltpu.make_async_copy(tab_v, tab, lsem.at[6])
+
     def prepare():
         right[PAIRS] = jnp.zeros((B, B), jnp.bfloat16)
         half[PAIRS] = jnp.zeros((B, B), jnp.bfloat16)
@@ -236,11 +249,9 @@
         tab_v[...] = jnp.zeros((8, B), jnp.int32)
         for n, row in enumerate(pair_tables(pairs_in[0:1, :], pairs_in[1:2, :], x, y, z)):
             tab_v[n : n + 1, :] = row
-        to_scalar = pltpu.make_async_copy(tab_v, tab, lsem.at[6])
         to_scalar.start()
         loads[3].wait()
         weight[...] = 1.0 / (diag[...] + 1.0)
-        to_scalar.wait()
 
     def scalars_sent(n, carry):
         for m in range(9):
@@ -269,9 +280,17 @@
             for m in far:
                 second_copy(j, m).start()
             forward_copy(j, 0).start()
-        for j in (0, *near):
+        for j in SHARED:
             for m in near:
                 second_copy(j, m).wait_recv()
+                share_copy(j, m).start()
+        for j in WHOLE:
+            for m in near:
+                second_copy(j, m).wait_recv()
+                forward_copy(j, m).start()
+        for j in SHARED:
+            for m in near:
+                share_copy(j, m).wait_recv()
                 forward_copy(j, m).start()
         for j in (0, *near):
             for m in (0, *near):
@@ -281,6 +300,7 @@
         def _():
             for j in range(1, 4):
                 pl.semaphore_signal(planes, inc=1, device_id=chip_at(j, 0, 0), device_id_type=MESH)
+            to_scalar.wait()
             loads[4].wait()
             loads[5].wait()
 
@@ -324,6 +344,8 @@
             for m in (0, *near):
                 if m:
                     second_copy(j, m).wait_send()
+                    if j in SHARED:
+                        share_copy(j, m).wait_send()
                 forward_copy(j, m).wait_send()
 
         def collect(n, carry):
@@ -454,6 +476,8 @@
             dma((16,)),
             dma((16,)),
             dma((16,)),
+            dma((16,)),
+            dma((16,)),
             dma((NSEC,)),
             dma((NSEC,)),
             dma((GROUPS,)),

time: 127 us -> 127 us (level)
  no operation moved by 1% of the time
where the time goes in v4:
time: 127 us
  Pallas kernels  125 us (98%)
  local copies, waits for them, and re-layouts  1.67 us (1%)
    pallas_call x1, Pallas kernels, shards(): pl.pallas_call(kernel, out_shape=jax.ShapeDtypeStruct((4, B, B), f32), in...  125 us

profile of v4, /device:TPU:1, one launch (start us, length us, event | category | flops | bytes accessed | tf_op | source)
XLA Modules:
  0.0 127.0 jit_solution(193898234585920838)
XLA Ops:
  0.0 125.3 %davidson.1 = f32[4,128,128]{2,1,0:T(8,128)} custom-call(s32[1,128]{1,0:T(1,128)} %bitcast.2, s32[1,128]{1,0:T(1,128)} %bitcast.3, f32[4,128,128]{2,1,0:T(8,128)} %psi_hbm.1, f32[4,128,128]{2,1,0:T(8,128)} %diag_hbm.1, bf16[128,128,128]{2,1,0:T(8,128)(2,1)} %left_hbm.1, bf16[128,128,128]{2,1,0:T(8,128)(2,1)} %right_hbm.1), custom_call_target="tpu_custom_call" | custom-call | flops 3221225472 | bytes 9437184 | tf_op jit(solution)/shard_map/davidson/pallas_call | solution.py:441
  125.4 1.7 %copy.8 = f32[4,128,128]{2,1,0:T(8,128)} copy(f32[4,128,128]{2,1,0:T(8,128)} %davidson.1) | data formatting | bytes 524288

commit v5 on v3

--- a/solution.py
+++ b/solution.py
@@ -151,8 +151,9 @@
         n = j * 4 + m
         return remote(block, block, fws.at[n], fwr.at[n], sibling)
 
-    def partial_copy(b):
-        return remote(psend.at[b], precv.at[b], pss.at[b], psr.at[b], sibling)
+    def partial_copy(h, part):
+        at, four = 2 * h + part, pl.ds(4 * part, 4)
+        return remote(psend.at[h, four], precv.at[h, four], pss.at[at], psr.at[at], sibling)
 
     def line_sum_copy(g, kk):
         k = g * 4 + kk
@@ -196,11 +197,13 @@
             low, high = total[:H], total[H:]
             pown[h, i] = jnp.where(c == 0, low, high)
             psend[h, i] = jnp.where(c == 0, high, low)
-        partial_copy(h).start()
+            if i % 4 == 3:
+                partial_copy(h, i // 4).start()
 
     def send_lines(h):
-        partial_copy(h).wait()
         for i in range(EACH):
+            if i % 4 == 0:
+                partial_copy(h, i // 4).wait()
             both = pown[h, i] + precv[h, i]
             g, kk = 2 * h + i // 4, i % 4
             if kk == 3:
@@ -219,8 +222,9 @@
             plane_sum_copy(g).start()
 
     def send_straight(h):
-        partial_copy(h).wait()
         for i in range(EACH):
+            if i % 4 == 0:
+                partial_copy(h, i // 4).wait()
             both = pown[h, i] + precv[h, i]
             if isinstance(h, int) and h == TURNS - 1 and i == EACH - 1:
                 acc[...] = both

time: 127 us -> 130 us (1.024)
  Pallas kernels: 125 us -> 129 us
    pallas_call x1, Pallas kernels: 125 us -> 129 us  [shards(): pl.pallas_call(kernel, out_shape=jax.ShapeDtypeStruct((4, B, B), f32), in...]
where the time goes in v5:
time: 130 us
  Pallas kernels  129 us (99%)
  local copies, waits for them, and re-layouts  1.67 us (1%)
    pallas_call x1, Pallas kernels, shards(): pl.pallas_call(kernel, out_shape=jax.ShapeDtypeStruct((4, B, B), f32), in...  129 us

profile of v5, /device:TPU:1, one launch (start us, length us, event | category | flops | bytes accessed | tf_op | source)
XLA Modules:
  0.0 130.3 jit_solution(2506669312258107859)
XLA Ops:
  0.0 128.6 %davidson.1 = f32[4,128,128]{2,1,0:T(8,128)} custom-call(s32[1,128]{1,0:T(1,128)} %bitcast.2, s32[1,128]{1,0:T(1,128)} %bitcast.3, f32[4,128,128]{2,1,0:T(8,128)} %psi_hbm.1, f32[4,128,128]{2,1,0:T(8,128)} %diag_hbm.1, bf16[128,128,128]{2,1,0:T(8,128)(2,1)} %left_hbm.1, bf16[128,128,128]{2,1,0:T(8,128)(2,1)} %right_hbm.1), custom_call_target="tpu_custom_call" | custom-call | flops 3221225472 | bytes 9437184 | tf_op jit(solution)/shard_map/davidson/pallas_call | solution.py:423
  128.6 1.7 %copy.8 = f32[4,128,128]{2,1,0:T(8,128)} copy(f32[4,128,128]{2,1,0:T(8,128)} %davidson.1) | data formatting | bytes 524288
